TPU v7x, 128 devices: a whole 4x4x4 slice. The times are simulated.
128 devices in a mesh: rep: 4 (over z_hi, core), fsdp: 32 (over y, x, z_lo).
Axes of the slice: x: 4, y: 4, z: 4 (z_hi: 2, z_lo: 2; z = z_hi * 2 + z_lo), core: 2. Of those that a mesh axis runs over, the one named last changes fastest.
Arguments:
- layer_input: bfloat16 [65536, 8192], P(('rep', 'fsdp')), may hold values from -0.1875 to 0.1875
- out_grad: bfloat16 [65536, 512], P(('rep', 'fsdp')), may hold values from -6 to 6
- master: float32 [4, 8192, 512], P('rep', 'fsdp'), may hold values from -0.0625 to 0.0625
- first_moment: float32 [4, 8192, 512], P('rep', 'fsdp'), may hold values from -6 to 6
- second_moment: float32 [4, 8192, 512], P('rep', 'fsdp'), may hold values from 0.1 to 10
- anchor: float32 [8192, 512], P('fsdp'), may hold values from -0.0625 to 0.0625
- outer_moment: float32 [8192, 512], P('fsdp'), may hold values from -0.06 to 0.06
Outputs:
- input_grad: bfloat16 [65536, 8192], P(('rep', 'fsdp'))
- master_out: float32 [4, 8192, 512], P('rep', 'fsdp')
- first_out: float32 [4, 8192, 512], P('rep', 'fsdp')
- second_out: float32 [4, 8192, 512], P('rep', 'fsdp')
- anchor_out: float32 [8192, 512], P('fsdp')
- outer_out: float32 [8192, 512], P('fsdp')
All inputs are finite; a program needn't handle non-finite values.
Results may differ from a plain program's by a relative error of at most 0.0049.
Values may be sent and summed in bfloat16 or wider, within the bound.
A program may use at most 128 MiB of HBM per device.

v0:
```python
import jax
import jax.numpy as jnp
from jax import lax
from jax.sharding import PartitionSpec as P

beta_one = 0.9
beta_two = 0.95
bias_one = 1.0 - 0.9**20
bias_two = 1.0 - 0.95**20


def contract_first(left_side, right_side):
    return lax.dot_general(
        left_side, right_side, (((0,), (0,)), ((), ())), preferred_element_type=jnp.float32
    )


def outer_update(anchor_block, moment_block, summed):
    delta = anchor_block - summed / lax.axis_size("rep")
    outer_new = 0.9 * moment_block + delta
    anchor_new = anchor_block - 0.7 * (0.9 * outer_new + delta)
    return (anchor_new, outer_new)


def on_device(layer_input, out_grad, master, first_moment, second_moment, anchor, outer_moment):
    master_local = master[0]
    weights = master_local.astype(jnp.bfloat16)
    input_grad = lax.dot_general(
        out_grad,
        lax.all_gather(weights, "fsdp", axis=0, tiled=True),
        (((1,), (1,)), ((), ())),
        preferred_element_type=jnp.float32,
    ).astype(jnp.bfloat16)
    gradient = lax.psum_scatter(
        contract_first(layer_input, out_grad), "fsdp", scatter_dimension=0, tiled=True
    )
    first_new = beta_one * first_moment[0] + (1.0 - beta_one) * gradient
    second_new = beta_two * second_moment[0] + (1.0 - beta_two) * gradient * gradient
    update = first_new / bias_one / (jnp.sqrt(second_new / bias_two) + 1e-08)
    inner = master_local - 0.002 * (update + 0.1 * master_local)
    summed = lax.psum(master_local, "rep")
    anchor_new, outer_new = outer_update(anchor, outer_moment, summed)
    master_new = 0.5 * inner + 0.5 * anchor_new
    return (input_grad, master_new[None], first_new[None], second_new[None], anchor_new, outer_new)


def solution(mesh):
    return jax.shard_map(
        on_device,
        mesh=mesh,
        in_specs=(
            P(("rep", "fsdp"), None),
            P(("rep", "fsdp"), None),
            P("rep", "fsdp", None),
            P("rep", "fsdp", None),
            P("rep", "fsdp", None),
            P("fsdp", None),
            P("fsdp", None),
        ),
        out_specs=(
            P(("rep", "fsdp"), None),
            P("rep", "fsdp", None),
            P("rep", "fsdp", None),
            P("rep", "fsdp", None),
            P("fsdp", None),
            P("fsdp", None),
        ),
        check_vma=False,
    )
```

profile of v0, /device:TPU:0, one launch (start us, length us, event | category | flops | bytes accessed | tf_op | source)
XLA Modules:
  0.0 583.9 jit_solution(11879235983313198352)
XLA Ops:
  8.0 0.0 copy-start
  8.0 0.0 all-gather.2.cloned.1.call-start
  8.1 1.8 bitcast_convert_fusion
  9.9 0.0 all-gather.2.cloned.1.call-update
  9.9 0.0 all-reduce.2.cloned.1.call-start
  10.0 0.5 all-reduce.2.cloned.1.call-update
  10.5 0.0 reduce-scatter.2.cloned.1.call-start
  10.5 0.0 copy-done
  10.5 11.7 %fusion.3 = f32[8192,512]{1,0:T(8,128)} fusion(bf16[512,8192]{1,0:T(8,128)(2,1)} %param.7, bf16[512,512]{1,0:T(8,128)(2,1)S(1)} %copy-done), kind=kOutput, calls=%fused_computation.11 | convolution fusion | flops 4294967296 | bytes 25690112 | tf_op jit(solution)/shard_map/dot_general | solution.py:13
  22.3 0.0 reduce-scatter.2.cloned.1.call-update
  22.3 0.0 copy-start.1
  22.3 0.0 copy-start.2
  22.3 0.0 copy-start.3
  22.3 0.0 copy-start.4
  22.3 0.0 copy-start.5
  22.3 188.7 %all-gather.2.cloned.1.call-done = bf16[8192,512]{1,0:T(8,128)(2,1)} async-done(((bf16[256,512]{1,0:T(8,128)(2,1)}), bf16[8192,512]{1,0:T(8,128)(2,1)}) %all-gather.2.cloned.1.call-update) | async-done | bytes 8388624 | tf_op jit(solution)/shard_map/all_gather | solution.py:30
  211.0 10.2 %convolution_convert_fusion = bf16[512,8192]{1,0:T(8,128)(2,1)} fusion(bf16[512,512]{1,0:T(8,128)(2,1)S(1)} %copy-done, bf16[8192,512]{1,0:T(8,128)(2,1)} %all-gather.2.cloned.1.call-done), kind=kOutput, calls=%fused_computation | convolution fusion | flops 4299161600 | bytes 17301504 | tf_op jit(solution)/shard_map/dot_general | solution.py:28
  221.2 0.0 all-reduce.2.cloned.1.call-done
  221.2 352.3 %reduce-scatter.2.cloned.1.call-done = f32[256,512]{1,0:T(8,128)} async-done(((f32[8192,512]{1,0:T(8,128)}), f32[256,512]{1,0:T(8,128)}) %reduce-scatter.2.cloned.1.call-update) | async-done | bytes 524304 | tf_op jit(solution)/shard_map/reduce_scatter | solution.py:34
  573.5 0.0 copy-done.1
  573.5 0.0 copy-done.2
  573.5 0.0 copy-done.3
  573.5 0.0 copy-done.4
  573.6 0.0 copy-done.5
  573.6 2.9 multiply_bitcast_fusion
Async XLA Ops:
  8.0 2.5 copy-start
  8.0 203.0 %all-gather.2.cloned.1.call-start = ((), (), s32[]{:S(2)}) async-start(), calls=%async_computation.1 | async-start | bytes 8650752 | tf_op jit(solution)/shard_map/all_gather | solution.py:30
  9.9 211.3 %all-reduce.2.cloned.1.call-start = ((), (), s32[]{:S(2)}) async-start(), calls=%async_computation.3 | async-start | bytes 1048576 | tf_op jit(solution)/shard_map/psum | solution.py:41
  10.5 563.1 %reduce-scatter.2.cloned.1.call-start = ((), (), s32[]{:S(2)}) async-start(), calls=%async_computation.2 | async-start | bytes 17301504 | tf_op jit(solution)/shard_map/reduce_scatter | solution.py:34
  22.3 551.3 %copy-start.1 = (f32[1,256,512]{2,1,0:T(8,128)S(1)}, f32[1,256,512]{2,1,0:T(8,128)}, u32[]{:S(2)}) copy-start(f32[1,256,512]{2,1,0:T(8,128)} %param.9) | copy-start | bytes 1572868
  22.3 551.2 %copy-start.2 = (f32[1,256,512]{2,1,0:T(8,128)S(1)}, f32[1,256,512]{2,1,0:T(8,128)}, u32[]{:S(2)}) copy-start(f32[1,256,512]{2,1,0:T(8,128)} %param.10) | copy-start | bytes 1572868
  22.3 551.2 %copy-start.3 = (f32[1,256,512]{2,1,0:T(8,128)S(1)}, f32[1,256,512]{2,1,0:T(8,128)}, u32[]{:S(2)}) copy-start(f32[1,256,512]{2,1,0:T(8,128)} %param.11) | copy-start | bytes 1572868
  22.3 551.2 %copy-start.4 = (f32[256,512]{1,0:T(8,128)S(1)}, f32[256,512]{1,0:T(8,128)}, u32[]{:S(2)}) copy-start(f32[256,512]{1,0:T(8,128)} %param.12) | copy-start | bytes 1572868
  22.3 551.2 %copy-start.5 = (f32[256,512]{1,0:T(8,128)S(1)}, f32[256,512]{1,0:T(8,128)}, u32[]{:S(2)}) copy-start(f32[256,512]{1,0:T(8,128)} %param.13) | copy-start | bytes 1572868
Sparse Core Ops, SparseCore 0:
  11.1 199.9 all-gather.1
  213.4 360.0 reduce-scatter.1
Sparse Core Ops, SparseCore 1:
  12.9 76.9 all-reduce.1
where the time goes:
time: 584 us
  waiting for transfers between devices  542 us (93%)
  matrix products  21.9 us (4%)
  between operations  15.6 us (3%)
    reduce_scatter x1, waiting for transfers between devices, on_device(): lax.psum_scatter(contract_first(layer_input, out_grad), 'fsdp', scatter_d...  352 us
    all_gather x1, waiting for transfers between devices, on_device(): lax.all_gather(weights, 'fsdp', axis=0, tiled=True)  189 us
    dot_general x1, matrix products, contract_first(): lax.dot_general(left_side, right_side, (((0,), (0,)), ((), ())), preferre...  11.7 us
  transfers between devices with their start and end apart: 3, of which 2 were waited for; matrix products, arithmetic and copies ran while one was open for 4% of the time, Pallas kernels for 0%

commit v1 on v0

v1 whole, which is shorter than its diff:
```python
import functools

import jax
import jax.numpy as jnp
from jax import lax
from jax.experimental import pallas as pl
from jax.experimental.pallas import tpu as pltpu
from jax.sharding import PartitionSpec as P

MESH = pl.DeviceIdType.MESH
BF16 = jnp.bfloat16
F32 = jnp.float32

beta_one = 0.9
beta_two = 0.95
bias_one = 1.0 - 0.9**20
bias_two = 1.0 - 0.95**20

SHARD = 256
COLS = 512
TOK = 512
SIZE = {"y": 4, "x": 4, "z": 2}

PARTS = (
    (0, 176, 96, "yxz"),
    (176, 176, 96, "xyz"),
    (352, 80, 48, "zyx"),
    (432, 80, 48, "zxy"),
)


def ring_order(k):
    high, low = k // 2, k % 2
    return 2 - low + high - 2 * high * low


def offsets_of(dims, k):
    found = {}
    for d in reversed(dims):
        at = k % SIZE[d]
        k = k // SIZE[d]
        found[d] = ring_order(at) if SIZE[d] == 4 else 1 - at
    return found


def count_of(dims):
    total = 1
    for d in dims:
        total *= SIZE[d]
    return total


def slot_of(dims, offsets):
    at = 0
    for d in dims:
        at = at * SIZE[d] + offsets[d]
    return at


def loop(count, body):
    if count == 1:
        body(0)
    else:
        lax.fori_loop(0, count, lambda k, c: (body(k), c)[1], 0)


class Layout:
    def __init__(self):
        self.names, self.shapes = [], []

    def add(self, name, shape):
        self.names.append(name)
        self.shapes.append(shape)


def layout():
    own = Layout()
    own.add("rows", pltpu.VMEM((4, TOK, 8 * SHARD), BF16))
    own.add("grad", pltpu.VMEM((TOK, COLS), BF16))
    own.add("grad_t", pltpu.VMEM((COLS, TOK), BF16))
    own.add("mast", pltpu.VMEM((SHARD, COLS), F32))
    own.add("weight", pltpu.VMEM((32, COLS, SHARD), BF16))
    own.add("product", pltpu.VMEM((32, TOK, SHARD), BF16))
    own.add("total", pltpu.VMEM((SHARD, COLS), F32))
    own.add("in_sem", pltpu.SemaphoreType.DMA((8,)))
    own.add("out_sem", pltpu.SemaphoreType.DMA((33,)))
    for p, (_, n, _, order) in enumerate(PARTS):
        for s in range(3):
            m = count_of(order[s + 1 :])
            kinds, bufs = (4, 3) if order[s] != "z" else (1, 1)
            own.add(f"send{p}{s}", pltpu.VMEM((bufs, m, n, SHARD), BF16))
            own.add(f"recv{p}{s}", pltpu.VMEM((bufs, m, n, SHARD), BF16))
            for what in ("rs", "rr", "gs", "gr"):
                own.add(f"{what}{p}{s}", pltpu.SemaphoreType.DMA((kinds, m)))
    return own


def kernel(names, rows_hbm, grad_hbm, mast_hbm, out_hbm, total_hbm, *refs):
    ref = dict(zip(names, refs))
    rep, fsdp = lax.axis_index("rep"), lax.axis_index("fsdp")
    me = {"y": fsdp // 8, "x": fsdp // 2 % 4, "z": fsdp % 2}

    def neighbour(d, step):
        at = dict(me)
        at[d] = (me[d] + step) % SIZE[d]
        return (rep, (at["y"] * 4 + at["x"]) * 2 + at["z"])

    to = {"+y": neighbour("y", 1), "-y": neighbour("y", 3), "+x": neighbour("x", 1), "-x": neighbour("x", 3), "z": neighbour("z", 1)}

    row_copies = []
    for k in range(4):
        y = (me["y"] + (2, 1, 3, 0)[k]) % 4
        row_copies.append(
            pltpu.make_async_copy(
                rows_hbm.at[:, pl.ds(pl.multiple_of(y * (8 * SHARD), 8 * SHARD), 8 * SHARD)],
                ref["rows"].at[y],
                ref["in_sem"].at[k],
            )
        )
    mast_copy = pltpu.make_async_copy(mast_hbm, ref["mast"], ref["in_sem"].at[4])
    grad_copy = pltpu.make_async_copy(grad_hbm, ref["grad"], ref["in_sem"].at[5])
    mast_copy.start()
    grad_copy.start()
    for copy in row_copies:
        copy.start()

    barrier = pltpu.get_barrier_semaphore()
    for target in to.values():
        pl.semaphore_signal(barrier, inc=1, device_id=target, device_id_type=MESH)

    mast_copy.wait()
    ref["weight"][0] = jnp.transpose(ref["mast"][...]).astype(BF16)
    pl.semaphore_wait(barrier, len(to))

    def remote(src, dst, send_sem, recv_sem, target):
        return pltpu.make_async_remote_copy(
            src_ref=src, dst_ref=dst, send_sem=send_sem, recv_sem=recv_sem, device_id=target, device_id_type=MESH
        )

    def weight_at(offsets, first, count):
        return ref["weight"].at[slot_of("yxz", offsets), pl.ds(first, count)]

    def gather_dims(p, s):
        return PARTS[p][3][s + 1 :]

    def gather_copy(p, s, inner, kind):
        first, n, low, order = PARTS[p]
        d, dims = order[s], gather_dims(p, s)
        base = {"y": 0, "x": 0, "z": 0, **inner}
        slot = slot_of(dims, inner)
        if d == "z":
            src, dst, a, c, target = 0, 1, first, n, to["z"]
        else:
            src, dst, a, c, target = (
                (0, 3, first, n, to["+" + d]),
                (0, 1, first, n, to["-" + d]),
                (3, 2, first, low, to["+" + d]),
                (1, 2, first + low, n - low, to["-" + d]),
            )[kind]
        return remote(
            weight_at({**base, d: src}, a, c),
            weight_at({**base, d: dst}, a, c),
            ref[f"gs{p}{s}"].at[kind, slot],
            ref[f"gr{p}{s}"].at[kind, slot],
            target,
        )

    def gather_send(p, s, inner):
        for kind in range(1 if PARTS[p][3][s] == "z" else 2):
            gather_copy(p, s, inner, kind).start()

    def gather_pass(p, s, inner):
        for kind in (0, 1):
            gather_copy(p, s, inner, kind).wait_recv()
            gather_copy(p, s, inner, kind + 2).start()

    def gather_far(p, s, inner):
        for kind in (2, 3):
            gather_copy(p, s, inner, kind).wait_recv()

    def own_tile(p, o):
        first, n = PARTS[p][:2]
        y, x, z = [(me[d] + o[d]) % SIZE[d] for d in "yxz"]
        column = pl.multiple_of((x * 2 + z) * SHARD, SHARD)
        return jnp.dot(
            ref["grad_t"][first : first + n, :],
            ref["rows"][y, :, pl.ds(column, SHARD)],
            preferred_element_type=F32,
        )

    def reduce_copy(p, s, inner, kind):
        _, n, low, order = PARTS[p]
        d = order[s]
        slot = slot_of(order[s + 1 :], inner)
        if d == "z":
            buf, a, c, target = 0, 0, n, to["z"]
        else:
            buf, a, c, target = (
                (0, 0, low, to["+" + d]),
                (0, low, n - low, to["-" + d]),
                (1, 0, n, to["+" + d]),
                (2, 0, n, to["-" + d]),
            )[kind]
        return remote(
            ref[f"send{p}{s}"].at[buf, slot, pl.ds(a, c)],
            ref[f"recv{p}{s}"].at[buf, slot, pl.ds(a, c)],
            ref[f"rs{p}{s}"].at[kind, slot],
            ref[f"rr{p}{s}"].at[kind, slot],
            target,
        )

    def summed(p, s, offsets):
        if s == 0:
            return own_tile(p, offsets)
        d = PARTS[p][3][s - 1]
        dims = PARTS[p][3][s:]
        inner = {e: offsets[e] for e in dims}
        value = summed(p, s - 1, {**offsets, d: 0})
        slot = slot_of(dims, inner)
        for kind, buf in ((0, 0),) if d == "z" else ((2, 1), (3, 2)):
            reduce_copy(p, s - 1, inner, kind).wait_recv()
            value = value + ref[f"recv{p}{s - 1}"][buf, slot].astype(F32)
        return value

    def reduce_far(p, s, inner):
        d = PARTS[p][3][s]
        value = summed(p, s, {**inner, d: 1 if d == "z" else 2})
        ref[f"send{p}{s}"][0, slot_of(PARTS[p][3][s + 1 :], inner)] = value.astype(BF16)
        for kind in range(1 if d == "z" else 2):
            reduce_copy(p, s, inner, kind).start()

    def reduce_near(p, s, inner):
        _, n, low, order = PARTS[p]
        d = order[s]
        slot = slot_of(order[s + 1 :], inner)
        for kind, offset, buf, a, c in ((0, 1, 1, 0, low), (1, 3, 2, low, n - low)):
            value = summed(p, s, {**inner, d: offset})
            reduce_copy(p, s, inner, kind).wait_recv()
            other = ref[f"recv{p}{s}"][0, slot, a : a + c].astype(F32)
            send = ref[f"send{p}{s}"]
            if kind == 0:
                send[buf, slot, :low] = (value[:low] + other).astype(BF16)
                send[buf, slot, low:] = value[low:].astype(BF16)
            else:
                send[buf, slot, :low] = value[:low].astype(BF16)
                send[buf, slot, low:] = (value[low:] + other).astype(BF16)
            reduce_copy(p, s, inner, kind + 2).start()

    def each(p, s, body, first=0, last=None):
        dims = PARTS[p][3][s + 1 :]
        count = count_of(dims)
        last = count if last is None else last
        loop(last - first, lambda k: body(p, s, offsets_of(dims, k + first)))

    def gather_inner(p, s, skip_own=True):
        dims = gather_dims(p, s)
        return dims, count_of(dims)

    def each_gather(p, s, body, first=0, last=None):
        dims = gather_dims(p, s)
        count = count_of(dims)
        last = count if last is None else last

        def step(k):
            inner, at = {}, k + first
            for d in reversed(dims):
                inner[d] = at % SIZE[d]
                at = at // SIZE[d]
            body(p, s, inner)

        loop(last - first, step)

    own = {"y": 0, "x": 0, "z": 0}

    def own_inner(p, s):
        return {d: 0 for d in gather_dims(p, s)}

    for p, s in ((0, 2), (1, 2), (2, 2), (3, 2), (2, 1), (3, 1), (0, 1), (1, 1), (0, 0), (1, 0), (2, 0), (3, 0)):
        gather_send(p, s, own_inner(p, s))

    grad_copy.wait()
    ref["grad_t"][...] = jnp.transpose(ref["grad"][...].astype(F32)).astype(BF16)
    for copy in row_copies:
        copy.wait()

    each(0, 0, reduce_far)
    each(1, 0, reduce_far)
    each(2, 0, reduce_far, 0, 8)
    each(3, 0, reduce_far, 0, 8)

    for p in (0, 1):
        gather_copy(p, 2, {}, 0).wait_recv()
        gather_send(p, 1, {"z": 1})
    for p in (2, 3):
        gather_pass(p, 2, {})

    each(2, 0, reduce_far, 8, 16)
    each(3, 0, reduce_far, 8, 16)
    each(0, 0, reduce_near)
    each(1, 0, reduce_near)

    def pass_then_send(p, s, inner):
        gather_pass(p, s, inner)
        d = PARTS[p][3][s]
        for offset in (1, 3):
            gather_send(p, s - 1, {**inner, d: offset})

    def far_then_send(p, s, inner):
        gather_far(p, s, inner)
        gather_send(p, s - 1, {**inner, PARTS[p][3][s]: 2})

    for p in (0, 1):
        gather_send(p, 0, {PARTS[p][3][1]: 0, "z": 1})
    for p in (0, 1):
        for z in (0, 1):
            pass_then_send(p, 1, {"z": z})
    for p in (2, 3):
        d = PARTS[p][3][2]
        for offset in (1, 3):
            gather_send(p, 1, {d: offset})
            gather_send(p, 0, {d: offset, PARTS[p][3][1]: 0})
        gather_far(p, 2, {})
        gather_send(p, 1, {d: 2})
        gather_send(p, 0, {d: 2, PARTS[p][3][1]: 0})
    for p in (0, 1):
        for z in (0, 1):
            far_then_send(p, 1, {"z": z})

    for p in (2, 3):
        each(p, 1, reduce_far)
    for p in (2, 3):
        each(p, 1, reduce_near)
    for p in (2, 3):
        each_gather(p, 1, pass_then_send)

    for p in (0, 1):
        each(p, 1, reduce_far)
    for p in (2, 3):
        each(p, 2, reduce_far)
    for p in (0, 1):
        each(p, 1, reduce_near)
    for p in (2, 3):
        each(p, 2, reduce_near)
    for p in (2, 3):
        each_gather(p, 1, far_then_send)
    for p in (0, 1):
        each(p, 2, reduce_far)
    for p in (0, 1, 2, 3):
        first, n = PARTS[p][:2]
        value = summed(p, 3, dict(own))
        ref["grad_sum"][first : first + n, :] = value
    ref["total"][...] = jnp.transpose(ref["grad_sum"][...])
    total_copy = pltpu.make_async_copy(ref["total"], total_hbm, ref["out_sem"].at[32])
    total_copy.start()

    for p in (0, 1):
        each_gather(p, 0, gather_pass)

    def product_copy(o):
        y, x, z = [(me[d] + o[d]) % SIZE[d] for d in "yxz"]
        column = pl.multiple_of(((y * 4 + x) * 2 + z) * SHARD, SHARD)
        slot = slot_of("yxz", o)
        return pltpu.make_async_copy(ref["product"].at[slot], out_hbm.at[:, pl.ds(column, SHARD)], ref["out_sem"].at[slot])

    def multiply(o):
        slot = slot_of("yxz", o)
        ref["product"][slot] = jnp.dot(ref["grad"][...], ref["weight"][slot], preferred_element_type=F32).astype(BF16)
        product_copy(o).start()

    def near(k):
        return k + k // 2

    loop(9, lambda k: multiply({"y": near(k // 3), "x": near(k % 3), "z": 0}))

    def along_z(o):
        for p in (2, 3):
            gather_copy(p, 0, {"y": o["y"], "x": o["x"]}, 0).wait_recv()

    def near_z(k):
        o = {"y": near(k // 3), "x": near(k % 3), "z": 1}
        along_z(o)
        multiply(o)

    loop(9, near_z)

    def far_x(z):
        def step(k):
            o = {"y": near(k), "x": 2, "z": z}
            gather_far(1, 0, {"y": o["y"], "z": z})
            if z:
                along_z(o)
            multiply(o)

        loop(3, step)

    def far_y(z):
        def step(k):
            o = {"y": 2, "x": near(k), "z": z}
            gather_far(0, 0, {"x": o["x"], "z": z})
            if z:
                along_z(o)
            multiply(o)

        loop(3, step)

    for z in (0, 1):
        far_x(z)
        far_y(z)
    for z in (0, 1):
        o = {"y": 2, "x": 2, "z": z}
        gather_far(0, 0, {"x": 2, "z": z})
        gather_far(1, 0, {"y": 2, "z": z})
        if z:
            along_z(o)
        multiply(o)

    for p in range(4):
        for s in range(3):
            for kind in range(1 if PARTS[p][3][s] == "z" else 4):
                each_gather(p, s, lambda p, s, inner: gather_copy(p, s, inner, kind).wait_send())
                each_gather(p, s, lambda p, s, inner: reduce_copy(p, s, inner, kind).wait_send())
    total_copy.wait()

    def finish(k):
        product_copy({"y": k // 8, "x": k // 2 % 4, "z": k % 2}).wait()

    loop(32, finish)


def exchange(layer_input, out_grad, master_local):
    own = layout()
    own.add("grad_sum", pltpu.VMEM((COLS, SHARD), F32))
    return pl.pallas_call(
        functools.partial(kernel, tuple(own.names)),
        out_shape=(
            jax.ShapeDtypeStruct((TOK, 32 * SHARD), BF16),
            jax.ShapeDtypeStruct((SHARD, COLS), F32),
        ),
        in_specs=[pl.BlockSpec(memory_space=pltpu.HBM)] * 3,
        out_specs=[pl.BlockSpec(memory_space=pltpu.HBM)] * 2,
        scratch_shapes=own.shapes,
        compiler_params=pltpu.CompilerParams(collective_id=0, has_side_effects=True, vmem_limit_bytes=60 << 20),
        cost_estimate=pl.CostEstimate(flops=2 * 2 * TOK * COLS * 32 * SHARD, bytes_accessed=20 << 20, transcendentals=0),
    )(layer_input, out_grad, master_local)


def outer_update(anchor_block, moment_block, summed):
    delta = anchor_block - summed / lax.axis_size("rep")
    outer_new = 0.9 * moment_block + delta
    anchor_new = anchor_block - 0.7 * (0.9 * outer_new + delta)
    return (anchor_new, outer_new)


def on_device(layer_input, out_grad, master, first_moment, second_moment, anchor, outer_moment):
    master_local = master[0]
    summed = lax.psum(master_local, "rep")
    input_grad, gradient = exchange(layer_input, out_grad, master_local)
    first_new = beta_one * first_moment[0] + (1.0 - beta_one) * gradient
    second_new = beta_two * second_moment[0] + (1.0 - beta_two) * gradient * gradient
    update = first_new / bias_one / (jnp.sqrt(second_new / bias_two) + 1e-08)
    inner = master_local - 0.002 * (update + 0.1 * master_local)
    anchor_new, outer_new = outer_update(anchor, outer_moment, summed)
    master_new = 0.5 * inner + 0.5 * anchor_new
    return (input_grad, master_new[None], first_new[None], second_new[None], anchor_new, outer_new)


def solution(mesh):
    return jax.shard_map(
        on_device,
        mesh=mesh,
        in_specs=(
            P(("rep", "fsdp"), None),
            P(("rep", "fsdp"), None),
            P("rep", "fsdp", None),
            P("rep", "fsdp", None),
            P("rep", "fsdp", None),
            P("fsdp", None),
            P("fsdp", None),
        ),
        out_specs=(
            P(("rep", "fsdp"), None),
            P("rep", "fsdp", None),
            P("rep", "fsdp", None),
            P("rep", "fsdp", None),
            P("fsdp", None),
            P("fsdp", None),
        ),
        check_vma=False,
    )
```

time: 584 us -> 138 us (0.24)
  waiting for transfers between devices: 542 us -> 0.7 us
  Pallas kernels: 0 us -> 112 us
  matrix products: 21.9 us -> 0 us
  local copies, waits for them, and re-layouts: 0.04 us -> 7.79 us
    reduce_scatter x1 -> x0, waiting for transfers between devices: 352 us -> none  [on_device(): lax.psum_scatter(contract_first(layer_input, out_grad), 'fsdp', scatter_d...]
    all_gather x1 -> x0, waiting for transfers between devices: 189 us -> none  [on_device(): lax.all_gather(weights, 'fsdp', axis=0, tiled=True)]
    pallas_call x0 -> x1, Pallas kernels: none -> 112 us  [exchange(): pl.pallas_call(functools.partial(kernel, tuple(own.names)), out_shape=(ja...]
    dot_general x2 -> x0, matrix products: 21.9 us -> none  [the longest x1 11.7 us: contract_first(): lax.dot_general(left_side, right_side, (((0,), (0,)), ((), ())), preferre...]
    unnamed x12 -> x11, local copies, waits for them, and re-layouts: 0.04 us -> 7.79 us
  transfers between devices with their start and end apart: 3 -> 1, of which waited for: 2 -> 0; matrix products, arithmetic and copies ran while one was open for 4% -> 0% of each run, Pallas kernels for 0% -> 81%
where the time goes in v1:
time: 138 us
  Pallas kernels  112 us (81%)
  between operations  14.1 us (10%)
  local copies, waits for them, and re-layouts  7.79 us (6%)
  other arithmetic  2.91 us (2%)
    pallas_call x1, Pallas kernels, exchange(): pl.pallas_call(functools.partial(kernel, tuple(own.names)), out_shape=(ja...  112 us
    unnamed x11, local copies, waits for them, and re-layouts  7.79 us
    broadcast_in_dim x1, other arithmetic, on_device(): master_new[None]  2.91 us
  transfers between devices with their start and end apart: 1, of which 0 were waited for; matrix products, arithmetic and copies ran while one was open for 0% of the time, Pallas kernels for 81%

profile of v1, /device:TPU:0, one launch (start us, length us, event | category | flops | bytes accessed | tf_op | source)
XLA Modules:
  0.0 137.8 jit_solution(9552522386251664026)
XLA Ops:
  7.2 0.0 all-reduce.2.cloned.1.call-start
  7.2 0.7 all-reduce.2.cloned.1.call-update
  7.9 0.0 copy-start
  7.9 0.0 copy-start.1
  7.9 0.0 copy-start.2
  7.9 0.0 copy-start.3
  7.9 0.0 copy-start.4
  8.0 112.2 %shard_map.118 = (bf16[512,8192]{1,0:T(8,128)(2,1)}, f32[256,512]{1,0:T(8,128)}) custom-call(bf16[512,8192]{1,0:T(8,128)(2,1)} %rows_hbm.1, bf16[512,512]{1,0:T(8,128)(2,1)} %grad_hbm.1, f32[256,512]{1,0:T(8,128)} %bitcast.21), custom_call_target="tpu_custom_call" | custom-call | flops 8589934592 | bytes 20971520 | tf_op jit(solution)/shard_map/pallas_call | solution.py:433
  120.1 0.0 all-reduce.2.cloned.1.call-done
  120.2 0.0 copy-done
  120.2 0.0 copy-done.1
  120.2 0.0 copy-done.2
  120.2 0.0 copy-done.3
  120.2 0.0 copy-done.4
  120.2 2.9 %multiply_bitcast_fusion = (f32[1,256,512]{2,1,0:T(8,128)}, f32[256,512]{1,0:T(8,128)}, f32[256,512]{1,0:T(8,128)}, f32[1,256,512]{2,1,0:T(8,128)}, f32[1,256,512]{2,1,0:T(8,128)}) fusion(f32[256,512]{1,0:T(8,128)} %get-tuple-element.9, f32[1,256,512]{2,1,0:T(8,128)S(1)} %copy-done.1, f32[1,256,512]{2,1,0:T(8,128)S(1)} %copy-done.2, ...), kind=kLoop, calls=%fused_computation.3 | loop fusion | flops 3276800 | bytes 6291456 | tf_op jit(solution)/shard_map/broadcast_in_dim | solution.py:464
  123.1 7.8 %copy.15 = bf16[512,8192]{1,0:T(8,128)(2,1)} copy(bf16[512,8192]{1,0:T(8,128)(2,1)} %get-tuple-element.21) | data formatting | bytes 16777216
Async XLA Ops:
  7.2 113.0 %all-reduce.2.cloned.1.call-start = ((), (), s32[]{:S(2)}) async-start(), calls=%async_computation | async-start | bytes 1048576 | tf_op jit(solution)/shard_map/psum | solution.py:456
  7.9 112.3 %copy-start = (f32[1,256,512]{2,1,0:T(8,128)S(1)}, f32[1,256,512]{2,1,0:T(8,128)}, u32[]{:S(2)}) copy-start(f32[1,256,512]{2,1,0:T(8,128)} %param.9) | copy-start | bytes 1572868
  7.9 112.3 %copy-start.1 = (f32[1,256,512]{2,1,0:T(8,128)S(1)}, f32[1,256,512]{2,1,0:T(8,128)}, u32[]{:S(2)}) copy-start(f32[1,256,512]{2,1,0:T(8,128)} %param.10) | copy-start | bytes 1572868
  7.9 112.3 %copy-start.2 = (f32[1,256,512]{2,1,0:T(8,128)S(1)}, f32[1,256,512]{2,1,0:T(8,128)}, u32[]{:S(2)}) copy-start(f32[1,256,512]{2,1,0:T(8,128)} %param.11) | copy-start | bytes 1572868
  7.9 112.3 %copy-start.3 = (f32[256,512]{1,0:T(8,128)S(1)}, f32[256,512]{1,0:T(8,128)}, u32[]{:S(2)}) copy-start(f32[256,512]{1,0:T(8,128)} %param.12) | copy-start | bytes 1572868
  7.9 112.3 %copy-start.4 = (f32[256,512]{1,0:T(8,128)S(1)}, f32[256,512]{1,0:T(8,128)}, u32[]{:S(2)}) copy-start(f32[256,512]{1,0:T(8,128)} %param.13) | copy-start | bytes 1572868
Sparse Core Ops, SparseCore 0:
  10.5 49.1 all-reduce.1

commit v2 on v0

v2 whole, which is shorter than its diff:
```python
import functools

import jax
import jax.numpy as jnp
from jax import lax
from jax.experimental import pallas as pl
from jax.experimental.pallas import tpu as pltpu
from jax.sharding import PartitionSpec as P

MESH = pl.DeviceIdType.MESH
BF16 = jnp.bfloat16
F32 = jnp.float32

beta_one = 0.9
beta_two = 0.95
bias_one = 1.0 - 0.9**20
bias_two = 1.0 - 0.95**20

SHARD = 256
COLS = 512
TOK = 512
SIZE = {"y": 4, "x": 4, "z": 2}
SHARDS = tuple({"y": y, "x": x, "z": z} for y in range(4) for x in range(4) for z in range(2))

PARTS = (
    (0, 176, 96, 80, "yxz"),
    (176, 176, 80, 96, "xyz"),
    (352, 80, 32, 48, "zyx"),
    (432, 80, 48, 32, "zxy"),
)

RATE, DELAY = 47500.0, 2.0
DOT, PRODUCT, ADD, SEND = 0.33, 0.31, 0.0005, 0.03


def count_of(dims):
    total = 1
    for d in dims:
        total *= SIZE[d]
    return total


def slot_of(dims, offsets):
    at = 0
    for d in dims:
        at = at * SIZE[d] + offsets[d]
    return at


def choices(dims):
    found = [{}]
    for d in dims:
        found = [{**o, d: k} for o in found for k in range(SIZE[d])]
    return found


def reduce_token(p, s, inner, kind):
    return ("reduce", p, s, slot_of(PARTS[p][4][s + 1 :], inner), kind)


def gather_token(p, s, inner, kind):
    return ("gather", p, s, slot_of(PARTS[p][4][s + 1 :], inner), kind)


def links_of(d):
    return ("z",) if d == "z" else ("+" + d, "-" + d)


def make_tasks():
    tasks = []

    def add(name, needs, time, sends, rank):
        tasks.append((name, tuple(needs), time + SEND * len(sends), tuple(sends), rank))

    def term_needs(p, s, o):
        order = PARTS[p][4]
        needs = [("dot", slot_of("yxz", o))]
        for t in range(s):
            inner = {e: o[e] for e in order[t + 1 :]}
            needs += [reduce_token(p, t, inner, k) for k in ((0,) if order[t] == "z" else (2, 3))]
        return needs

    for o in SHARDS:
        sends = []
        for p, (_, n, low, _, order) in enumerate(PARTS):
            d, inner = order[0], {e: o[e] for e in order[1:]}
            if d == "z" and o["z"] == 1:
                sends.append(("z", n * 512, reduce_token(p, 0, inner, 0)))
            if d != "z" and o[d] == 2:
                sends.append(("+" + d, low * 512, reduce_token(p, 0, inner, 0)))
                sends.append(("-" + d, (n - low) * 512, reduce_token(p, 0, inner, 1)))
        far = (o["y"] == 2) + (o["x"] == 2)
        add(("dot", slot_of("yxz", o)), [], DOT, sends, 22 - 2 * far - o["z"])
    for p, (_, n, low, glow, order) in enumerate(PARTS):
        for s in range(3):
            d = order[s]
            for inner in choices(order[s + 1 :]):
                o = {**{e: 0 for e in order[:s]}, **inner}
                at = slot_of(order[s + 1 :], inner)
                if s:
                    sizes = (n,) if d == "z" else (low, n - low)
                    sends = [(link, size * 512, reduce_token(p, s, inner, k)) for k, (link, size) in enumerate(zip(links_of(d), sizes))]
                    add(("far", p, s, at), term_needs(p, s, {**o, d: 1 if d == "z" else 2}), ADD * n * s, sends, 10)
                if d != "z":
                    for k, link in enumerate(links_of(d)):
                        needs = term_needs(p, s, {**o, d: 1 + 2 * k}) + [reduce_token(p, s, inner, k)]
                        add(("near", p, s, at, k), needs, ADD * n * (s + 1), [(link, n * 512, reduce_token(p, s, inner, k + 2))], 10)
        add(("final", p), term_needs(p, 3, {"y": 0, "x": 0, "z": 0}), ADD * n * 4, [], 10)
    add(("total",), [("final", p) for p in range(len(PARTS))], 0.5, [], 10)

    arrivals = {slot: [] for slot in range(32)}
    for p, (_, n, _, low, order) in enumerate(PARTS):
        have = {0: ({"y": 0, "x": 0, "z": 0}, [])}
        for s in (2, 1, 0):
            d = order[s]
            rank = 30 if s == 0 else 0
            for o, needs in list(have.values()):
                inner = {e: o[e] for e in order[s + 1 :]}
                at = slot_of(order[s + 1 :], inner)
                token = [gather_token(p, s, inner, k) for k in range(4)]
                add(("send", p, s, at), needs, 0.0, [(link, n * 512, token[k]) for k, link in enumerate(links_of(d))], rank)
                if d == "z":
                    found = {1: [token[0]]}
                else:
                    add(("pass", p, s, at, 0), [token[0]], 0.0, [("+" + d, low * 512, token[2])], rank)
                    add(("pass", p, s, at, 1), [token[1]], 0.0, [("-" + d, (n - low) * 512, token[3])], rank)
                    found = {3: [token[0]], 1: [token[1]], 2: [token[2], token[3]]}
                for k, tokens in found.items():
                    shard = {**o, d: k}
                    have[slot_of("yxz", shard)] = (shard, tokens)
        for slot, (_, tokens) in have.items():
            arrivals[slot] += tokens
    for slot in range(32):
        add(("product", slot), arrivals[slot] + [("dot", k) for k in range(32)], PRODUCT, [], 90)

    add(("sum", 0), [], 0.0, [("core", SHARD * COLS * 2, ("sum", "in", 0))], 1)
    add(("sum", 1), [("sum", "in", 0)], 0.1, [("z", SHARD * COLS * 2, ("sum", "in", 1))], 11)
    add(("sum", 2), [("sum", "in", 1)], 0.1, [("core", SHARD * COLS * 2, ("sum", "in", 2))], 12)
    add(("sum", 3), [("sum", "in", 2)], 0.0, [], 80)
    return tasks


def in_order(tasks):
    now, done, free, order = 0.0, {}, {}, []
    left = sorted(tasks, key=lambda task: task[4])
    while left:
        ready, soonest = None, None
        for task in left:
            if all(token in done for token in task[1]):
                at = max([done[token] for token in task[1]], default=0.0)
                if at <= now:
                    ready = task
                    break
                soonest = at if soonest is None else min(soonest, at)
        if ready is None:
            now = soonest
            continue
        left.remove(ready)
        order.append(ready)
        now += ready[2]
        done[ready[0]] = now
        for link, size, token in ready[3]:
            rate = 12 * RATE if link == "core" else RATE
            free[link] = max(free.get(link, 0.0), now) + size / rate
            done[token] = free[link] + DELAY
    return order


class Layout:
    def __init__(self):
        self.names, self.shapes = [], []

    def add(self, name, shape):
        self.names.append(name)
        self.shapes.append(shape)


def layout():
    own = Layout()
    own.add("grad", pltpu.VMEM((TOK, COLS), BF16))
    own.add("grad_t", pltpu.VMEM((COLS, TOK), BF16))
    own.add("mast", pltpu.VMEM((SHARD, COLS), F32))
    own.add("weight", pltpu.VMEM((32, COLS, SHARD), BF16))
    own.add("term", pltpu.VMEM((32, COLS, SHARD), F32))
    own.add("sum_send", pltpu.VMEM((SHARD // 2, COLS), F32))
    own.add("sum_recv", pltpu.VMEM((2, SHARD // 2, COLS), F32))
    own.add("sum_ss", pltpu.SemaphoreType.DMA((3,)))
    own.add("sum_rs", pltpu.SemaphoreType.DMA((3,)))
    own.add("grad_sum", pltpu.VMEM((COLS, SHARD), F32))
    own.add("in_sem", pltpu.SemaphoreType.DMA((6,)))
    for p, (_, n, _, _, order) in enumerate(PARTS):
        for s in range(3):
            m = count_of(order[s + 1 :])
            kinds, bufs = (4, 3) if order[s] != "z" else (1, 1)
            own.add(f"send{p}{s}", pltpu.VMEM((bufs, m, n, SHARD), BF16))
            own.add(f"recv{p}{s}", pltpu.VMEM((bufs, m, n, SHARD), BF16))
            for what in ("rr", "gr"):
                own.add(f"{what}{p}{s}", pltpu.SemaphoreType.DMA((kinds, m)))
            for what in ("rs", "gs"):
                own.add(f"{what}{p}{s}", pltpu.SemaphoreType.DMA)
    return own


def kernel(names, rows_hbm, grad_hbm, mast_hbm, out_ref, total_ref, sum_ref, *refs):
    ref = dict(zip(names, refs))
    rep, fsdp = lax.axis_index("rep"), lax.axis_index("fsdp")
    me = {"y": fsdp // 8, "x": fsdp // 2 % 4, "z": fsdp % 2}
    core = rep % 2
    place = {d: [(me[d] + k) % SIZE[d] for k in range(SIZE[d])] for d in "yxz"}

    def device(y, x, z):
        return (rep, (y * 4 + x) * 2 + z)

    to = {
        "+y": device(place["y"][1], me["x"], me["z"]),
        "-y": device(place["y"][3], me["x"], me["z"]),
        "+x": device(me["y"], place["x"][1], me["z"]),
        "-x": device(me["y"], place["x"][3], me["z"]),
        "z": device(me["y"], me["x"], place["z"][1]),
        "core": (rep + 1 - 2 * core, fsdp),
        "far": ((rep + 2) % 4, fsdp),
    }

    barrier = pltpu.get_barrier_semaphore()
    for target in to.values():
        pl.semaphore_signal(barrier, inc=1, device_id=target, device_id_type=MESH)

    mast_copy = pltpu.make_async_copy(mast_hbm, ref["mast"], ref["in_sem"].at[4])
    grad_copy = pltpu.make_async_copy(grad_hbm, ref["grad"], ref["in_sem"].at[5])
    row_copies = []
    for k in range(4):
        columns = pl.ds(pl.multiple_of(place["y"][(2, 1, 3, 0)[k]] * (8 * SHARD), 8 * SHARD), 8 * SHARD)
        row_copies.append(pltpu.make_async_copy(rows_hbm.at[:, columns], out_ref.at[:, columns], ref["in_sem"].at[k]))
    for copy in (mast_copy, grad_copy, *row_copies):
        copy.start()

    def columns_of(o):
        y, x, z = [place[d][o[d]] for d in "yxz"]
        return pl.ds(pl.multiple_of(((y * 4 + x) * 2 + z) * SHARD, SHARD), SHARD)

    def remote(src, dst, send_sem, recv_sem, target):
        return pltpu.make_async_remote_copy(
            src_ref=src, dst_ref=dst, send_sem=send_sem, recv_sem=recv_sem, device_id=target, device_id_type=MESH
        )

    half = SHARD // 2
    mine = pl.ds(pl.multiple_of(core * half, half), half)
    other = pl.ds(pl.multiple_of((1 - core) * half, half), half)

    def sum_copy(k):
        src, dst, target = (
            (ref["mast"].at[other], ref["sum_recv"].at[0], to["core"]),
            (ref["sum_send"], ref["sum_recv"].at[1], to["far"]),
            (sum_ref.at[mine], sum_ref.at[mine], to["core"]),
        )[k]
        return remote(src, dst, ref["sum_ss"].at[k], ref["sum_rs"].at[k], target)

    def weight_at(offsets, first, count):
        return ref["weight"].at[slot_of("yxz", offsets), pl.ds(first, count)]

    def gather_copy(p, s, inner, kind):
        first, n, _, low, order = PARTS[p]
        d, dims = order[s], order[s + 1 :]
        base = {"y": 0, "x": 0, "z": 0, **inner}
        if d == "z":
            src, dst, a, c, link = 0, 1, first, n, "z"
        else:
            src, dst, a, c, link = (
                (0, 3, first, n, "+" + d),
                (0, 1, first, n, "-" + d),
                (3, 2, first, low, "+" + d),
                (1, 2, first + low, n - low, "-" + d),
            )[kind]
        return remote(
            weight_at({**base, d: src}, a, c),
            weight_at({**base, d: dst}, a, c),
            ref[f"gs{p}{s}"],
            ref[f"gr{p}{s}"].at[kind, slot_of(dims, inner)],
            to[link],
        )

    def reduce_copy(p, s, inner, kind):
        _, n, low, _, order = PARTS[p]
        d = order[s]
        slot = slot_of(order[s + 1 :], inner)
        if d == "z":
            buf, a, c, link = 0, 0, n, "z"
        else:
            buf, a, c, link = (
                (0, 0, low, "+" + d),
                (0, low, n - low, "-" + d),
                (1, 0, n, "+" + d),
                (2, 0, n, "-" + d),
            )[kind]
        return remote(
            ref[f"send{p}{s}"].at[buf, slot, pl.ds(a, c)],
            ref[f"recv{p}{s}"].at[buf, slot, pl.ds(a, c)],
            ref[f"rs{p}{s}"],
            ref[f"rr{p}{s}"].at[kind, slot],
            to[link],
        )

    def inner_of(p, s, at):
        return choices(PARTS[p][4][s + 1 :])[at]

    waited = set()

    def wait_for(token):
        if token in waited or token[0] not in ("reduce", "gather") and token[1] != "in":
            return
        waited.add(token)
        if token[0] == "sum":
            sum_copy(token[2]).wait_recv()
        else:
            _, p, s, at, kind = token
            (reduce_copy if token[0] == "reduce" else gather_copy)(p, s, inner_of(p, s, at), kind).wait_recv()

    def term(p, s, o):
        first, n, _, _, order = PARTS[p]
        value = ref["term"][slot_of("yxz", o), first : first + n, :]
        for t in range(s):
            slot = slot_of(order[t + 1 :], o)
            for buf in (0,) if order[t] == "z" else (1, 2):
                value = value + ref[f"recv{p}{t}"][buf, slot].astype(F32)
        return value

    def do_dot(slot):
        o = SHARDS[slot]
        value = jnp.dot(ref["grad_t"][...], out_ref[:, columns_of(o)], preferred_element_type=F32)
        for p, (first, n, _, _, order) in enumerate(PARTS):
            d, inner = order[0], {e: o[e] for e in order[1:]}
            piece = value[first : first + n, :]
            if o[d] == (1 if d == "z" else 2):
                ref[f"send{p}0"][0, slot_of(order[1:], inner)] = piece.astype(BF16)
                for kind in range(len(links_of(d))):
                    reduce_copy(p, 0, inner, kind).start()
            else:
                ref["term"][slot, first : first + n, :] = piece

    def do_far(p, s, at):
        order = PARTS[p][4]
        d, inner = order[s], inner_of(p, s, at)
        o = {**{e: 0 for e in order[:s]}, **inner, d: 1 if d == "z" else 2}
        ref[f"send{p}{s}"][0, at] = term(p, s, o).astype(BF16)
        for kind in range(len(links_of(d))):
            reduce_copy(p, s, inner, kind).start()

    def do_near(p, s, at, kind):
        _, n, low, _, order = PARTS[p]
        d, inner = order[s], inner_of(p, s, at)
        value = term(p, s, {**{e: 0 for e in order[:s]}, **inner, d: 1 + 2 * kind})
        send, recv = ref[f"send{p}{s}"], ref[f"recv{p}{s}"]
        for which, (a, b) in enumerate(((0, low), (low, n))):
            piece = value[a:b]
            if which == kind:
                piece = piece + recv[0, at, a:b].astype(F32)
            send[kind + 1, at, a:b] = piece.astype(BF16)
        reduce_copy(p, s, inner, kind + 2).start()

    def do_final(p):
        first, n = PARTS[p][:2]
        ref["grad_sum"][first : first + n, :] = term(p, 3, {"y": 0, "x": 0, "z": 0})

    def do_total():
        total_ref[...] = jnp.transpose(ref["grad_sum"][...])

    def do_send(p, s, at):
        for kind in range(len(links_of(PARTS[p][4][s]))):
            gather_copy(p, s, inner_of(p, s, at), kind).start()

    def do_pass(p, s, at, kind):
        gather_copy(p, s, inner_of(p, s, at), kind + 2).start()

    def do_product(slot):
        value = jnp.dot(ref["grad"][...], ref["weight"][slot], preferred_element_type=F32)
        out_ref[:, columns_of(SHARDS[slot])] = value.astype(BF16)

    def do_sum(k):
        if k == 1:
            ref["sum_send"][...] = ref["mast"][mine, :] + ref["sum_recv"][0]
        if k == 2:
            sum_ref[mine, :] = ref["sum_send"][...] + ref["sum_recv"][1]
        if k < 3:
            sum_copy(k).start()

    steps = {
        "dot": do_dot,
        "far": do_far,
        "near": do_near,
        "final": do_final,
        "total": do_total,
        "send": do_send,
        "pass": do_pass,
        "product": do_product,
        "sum": do_sum,
    }

    mast_copy.wait()
    ref["weight"][0] = jnp.transpose(ref["mast"][...]).astype(BF16)
    pl.semaphore_wait(barrier, len(to))

    loaded = False
    for name, needs, _, _, _ in in_order(make_tasks()):
        if name[0] == "dot" and not loaded:
            loaded = True
            grad_copy.wait()
            ref["grad_t"][...] = jnp.transpose(ref["grad"][...].astype(F32)).astype(BF16)
            for copy in row_copies:
                copy.wait()
        for token in needs:
            wait_for(token)
        with jax.named_scope(name[0]):
            steps[name[0]](*name[1:])

    for p, (first, n, _, _, order) in enumerate(PARTS):
        for s in range(3):
            send = ref[f"send{p}{s}"]
            remote(send, ref[f"recv{p}{s}"], ref[f"rs{p}{s}"], ref[f"rs{p}{s}"], to["z"]).wait_send()
            count = count_of(order[s + 1 :]) * (1 if order[s] == "z" else 3)
            block = ref["weight"].at[pl.ds(0, count), pl.ds(first, n)]
            remote(block, block, ref[f"gs{p}{s}"], ref[f"gs{p}{s}"], to["z"]).wait_send()
    for k in range(3):
        sum_copy(k).wait_send()


def exchange(layer_input, out_grad, master_local):
    own = layout()
    return pl.pallas_call(
        functools.partial(kernel, tuple(own.names)),
        out_shape=(
            pltpu.VMEM((TOK, 32 * SHARD), BF16),
            pltpu.VMEM((SHARD, COLS), F32),
            pltpu.VMEM((SHARD, COLS), F32),
        ),
        in_specs=[pl.BlockSpec(memory_space=pltpu.HBM)] * 3,
        out_specs=[pl.BlockSpec(memory_space=pltpu.VMEM)] * 3,
        scratch_shapes=own.shapes,
        compiler_params=pltpu.CompilerParams(collective_id=0, has_side_effects=True, vmem_limit_bytes=51 << 20),
        cost_estimate=pl.CostEstimate(flops=2 * 2 * TOK * COLS * 32 * SHARD, bytes_accessed=20 << 20, transcendentals=0),
    )(layer_input, out_grad, master_local)


def outer_update(anchor_block, moment_block, summed):
    delta = anchor_block - summed / lax.axis_size("rep")
    outer_new = 0.9 * moment_block + delta
    anchor_new = anchor_block - 0.7 * (0.9 * outer_new + delta)
    return (anchor_new, outer_new)


def on_device(layer_input, out_grad, master, first_moment, second_moment, anchor, outer_moment):
    master_local = master[0]
    input_grad, gradient, summed = exchange(layer_input, out_grad, master_local)
    first_new = beta_one * first_moment[0] + (1.0 - beta_one) * gradient
    second_new = beta_two * second_moment[0] + (1.0 - beta_two) * gradient * gradient
    update = first_new / bias_one / (jnp.sqrt(second_new / bias_two) + 1e-08)
    inner = master_local - 0.002 * (update + 0.1 * master_local)
    anchor_new, outer_new = outer_update(anchor, outer_moment, summed)
    master_new = 0.5 * inner + 0.5 * anchor_new
    return (input_grad, master_new[None], first_new[None], second_new[None], anchor_new, outer_new)


def solution(mesh):
    return jax.shard_map(
        on_device,
        mesh=mesh,
        in_specs=(
            P(("rep", "fsdp"), None),
            P(("rep", "fsdp"), None),
            P("rep", "fsdp", None),
            P("rep", "fsdp", None),
            P("rep", "fsdp", None),
            P("fsdp", None),
            P("fsdp", None),
        ),
        out_specs=(
            P(("rep", "fsdp"), None),
            P("rep", "fsdp", None),
            P("rep", "fsdp", None),
            P("rep", "fsdp", None),
            P("fsdp", None),
            P("fsdp", None),
        ),
        check_vma=False,
    )
```

time: 584 us -> 90.4 us (0.15)
  waiting for transfers between devices: 542 us -> 0 us
  Pallas kernels: 0 us -> 84.2 us
  matrix products: 21.9 us -> 0 us
  between operations: 15.6 us -> 0.69 us
    reduce_scatter x1 -> x0, waiting for transfers between devices: 352 us -> none  [on_device(): lax.psum_scatter(contract_first(layer_input, out_grad), 'fsdp', scatter_d...]
    all_gather x1 -> x0, waiting for transfers between devices: 189 us -> none  [on_device(): lax.all_gather(weights, 'fsdp', axis=0, tiled=True)]
    pallas_call x0 -> x1, Pallas kernels: none -> 84.2 us  [exchange(): pl.pallas_call(functools.partial(kernel, tuple(own.names)), out_shape=(pl...]
    dot_general x2 -> x0, matrix products: 21.9 us -> none  [the longest x1 11.7 us: contract_first(): lax.dot_general(left_side, right_side, (((0,), (0,)), ((), ())), preferre...]
  transfers between devices with their start and end apart: 3 -> 0, of which waited for: 2 -> 0; matrix products, arithmetic and copies ran while one was open for 4% -> 0% of each run, Pallas kernels for 0% -> 0%
where the time goes in v2:
time: 90.4 us; the launch traced here: 90.3 us
  Pallas kernels  84.2 us (93%)
  local copies, waits for them, and re-layouts  3.68 us (4%)
  other arithmetic  1.71 us (2%)
    pallas_call x1, Pallas kernels, exchange(): pl.pallas_call(functools.partial(kernel, tuple(own.names)), out_shape=(pl...  84.2 us
    unnamed x11, local copies, waits for them, and re-layouts  3.68 us

profile of v2, /device:TPU:0, one launch (start us, length us, event | category | flops | bytes accessed | tf_op | source)
XLA Modules:
  0.0 90.3 jit_solution(1177935914284962)
XLA Ops:
  0.6 84.2 %shard_map.118 = (bf16[512,8192]{1,0:T(8,128)(2,1)S(1)}, f32[256,512]{1,0:T(8,128)S(1)}, f32[256,512]{1,0:T(8,128)S(1)}) custom-call(bf16[512,8192]{1,0:T(8,128)(2,1)} %rows_hbm.1, bf16[512,512]{1,0:T(8,128)(2,1)} %grad_hbm.1, f32[256,512]{1,0:T(8,128)} %bitcast.20), custom_call_target="tpu_custom_call" | custom-call | flops 8589934592 | bytes 20971520 | tf_op jit(solution)/shard_map/pallas_call | solution.py:428
  84.9 0.0 copy-start
  84.9 0.0 copy-start.1
  84.9 0.0 copy-start.2
  84.9 0.0 copy-start.3
  84.9 0.0 copy-start.4
  84.9 3.6 %copy.14 = bf16[512,8192]{1,0:T(8,128)(2,1)} copy(bf16[512,8192]{1,0:T(8,128)(2,1)S(1)} %get-tuple-element.17) | data formatting | bytes 16777216
  88.6 0.0 copy-done
  88.6 0.0 copy-done.1
  88.6 0.0 copy-done.2
  88.6 0.0 copy-done.3
  88.6 0.0 copy-done.4
  88.6 1.7 %multiply_bitcast_fusion = (f32[1,256,512]{2,1,0:T(8,128)}, f32[256,512]{1,0:T(8,128)}, f32[256,512]{1,0:T(8,128)}, f32[1,256,512]{2,1,0:T(8,128)}, f32[1,256,512]{2,1,0:T(8,128)}) fusion(f32[256,512]{1,0:T(8,128)S(1)} %get-tuple-element.10, f32[1,256,512]{2,1,0:T(8,128)S(1)} %copy-done.1, f32[1,256,512]{2,1,0:T(8,128)S(1)} %copy-done.2, ...), kind=kLoop, calls=%fused_computation.3 | loop fusion | flops 3276800 | bytes 6291456 | tf_op jit(solution)/shard_map/broadcast_in_dim | solution.py:459
Async XLA Ops:
  84.9 3.7 %copy-start = (f32[1,256,512]{2,1,0:T(8,128)S(1)}, f32[1,256,512]{2,1,0:T(8,128)}, u32[]{:S(2)}) copy-start(f32[1,256,512]{2,1,0:T(8,128)} %param.9) | copy-start | bytes 1572868
  84.9 3.7 %copy-start.1 = (f32[1,256,512]{2,1,0:T(8,128)S(1)}, f32[1,256,512]{2,1,0:T(8,128)}, u32[]{:S(2)}) copy-start(f32[1,256,512]{2,1,0:T(8,128)} %param.10) | copy-start | bytes 1572868
  84.9 3.7 %copy-start.2 = (f32[1,256,512]{2,1,0:T(8,128)S(1)}, f32[1,256,512]{2,1,0:T(8,128)}, u32[]{:S(2)}) copy-start(f32[1,256,512]{2,1,0:T(8,128)} %param.11) | copy-start | bytes 1572868
  84.9 3.7 %copy-start.3 = (f32[256,512]{1,0:T(8,128)S(1)}, f32[256,512]{1,0:T(8,128)}, u32[]{:S(2)}) copy-start(f32[256,512]{1,0:T(8,128)} %param.12) | copy-start | bytes 1572868
  84.9 3.7 %copy-start.4 = (f32[256,512]{1,0:T(8,128)S(1)}, f32[256,512]{1,0:T(8,128)}, u32[]{:S(2)}) copy-start(f32[256,512]{1,0:T(8,128)} %param.13) | copy-start | bytes 1572868

commit v3 on v2

v3 whole, which is shorter than its diff:
```python
import functools

import jax
import jax.numpy as jnp
from jax import lax
from jax.experimental import pallas as pl
from jax.experimental.pallas import tpu as pltpu
from jax.sharding import PartitionSpec as P

MESH = pl.DeviceIdType.MESH
BF16 = jnp.bfloat16
F32 = jnp.float32

beta_one = 0.9
beta_two = 0.95
bias_one = 1.0 - 0.9**20
bias_two = 1.0 - 0.95**20

SHARD = 256
COLS = 512
TOK = 512
SIZE = {"y": 4, "x": 4, "z": 2}
SHARDS = tuple({"y": y, "x": x, "z": z} for y in range(4) for x in range(4) for z in range(2))

REDUCE = (
    (0, 176, 96, "yxz", (2, 2, 1)),
    (176, 176, 80, "xyz", (2, 2, 1)),
    (352, 80, 32, "zyx", (4, 2, 1)),
    (432, 80, 48, "zxy", (4, 2, 1)),
)
GATHER = (
    (0, 176, 80, "yxz", (2, 1, 1)),
    (176, 176, 96, "xyz", (2, 1, 1)),
    (352, 80, 48, "zyx", (4, 1, 1)),
    (432, 80, 32, "zxy", (4, 1, 1)),
)

RATE, MESSAGE, DELAY = 48500.0, 0.08, 1.5
DOT, PRODUCT, ADD, SEND = 0.40, 0.38, 0.0005, 0.02
AHEAD = 6.0


def count_of(dims):
    total = 1
    for d in dims:
        total *= SIZE[d]
    return total


def slot_of(dims, offsets):
    at = 0
    for d in dims:
        at = at * SIZE[d] + offsets[d]
    return at


def choices(dims):
    found = [{}]
    for d in dims:
        found = [{**o, d: k} for o in found for k in range(SIZE[d])]
    return found


def links_of(d):
    return ("z",) if d == "z" else ("+" + d, "-" + d)


def groups_of(parts, p, s):
    _, _, _, order, together = parts[p]
    inner = choices(order[s + 1 :])
    return [inner[k : k + together[s]] for k in range(0, len(inner), together[s])]


def block_of(p, s, buf, slot):
    order = REDUCE[p][3]
    sizes = [count_of(order[t + 1 :]) * (1 if order[t] == "z" else 3) for t in range(s)]
    return sum(sizes) + buf * count_of(order[s + 1 :]) + slot


def group_with(parts, p, s, o):
    _, _, _, order, together = parts[p]
    return slot_of(order[s + 1 :], o) // together[s]


def make_tasks():
    tasks = []

    def add(name, needs, time, sends, rank):
        tasks.append((name, tuple(dict.fromkeys(needs)), time + SEND * len(sends), tuple(sends), rank))

    def term_needs(p, s, o):
        order = REDUCE[p][3]
        needs = [("dot", slot_of("yxz", o))]
        for t in range(s):
            needs.append(("reduce", p, t, group_with(REDUCE, p, t, o), 0 if order[t] == "z" else 1))
        return needs

    for o in SHARDS:
        far = (o["y"] == 2) + (o["x"] == 2)
        add(("dot", slot_of("yxz", o)), [], DOT, [], 22 - 2 * far - o["z"])
    for p, (_, n, low, order, together) in enumerate(REDUCE):
        for s in range(3):
            d, g = order[s], together[s]
            for at, group in enumerate(groups_of(REDUCE, p, s)):
                zero = {e: 0 for e in order[:s]}
                sizes = (n,) if d == "z" else (low, n - low)
                sends = [(link, g * size * 512, ("reduce", p, s, at, 0)) for link, size in zip(links_of(d), sizes)]
                needs = [t for o in group for t in term_needs(p, s, {**zero, **o, d: 1 if d == "z" else 2})]
                add(("far", p, s, at), needs, ADD * n * s * g, sends, 10)
                if d != "z":
                    needs = [t for o in group for k in (1, 3) for t in term_needs(p, s, {**zero, **o, d: k})] + [("reduce", p, s, at, 0)]
                    sends = [(link, g * n * 512, ("reduce", p, s, at, 1)) for link in links_of(d)]
                    add(("near", p, s, at), needs, ADD * n * (s + 1) * g * 2, sends, 10)
        add(("final", p), term_needs(p, 3, {"y": 0, "x": 0, "z": 0}), ADD * n * 4, [], 10)

    arrivals = {slot: [] for slot in range(32)}
    for p, (_, n, low, order, together) in enumerate(GATHER):
        have = {0: []}
        for s in (2, 1, 0):
            d, g = order[s], together[s]
            rank = 30 if s == 0 else 0
            zero = {e: 0 for e in order[: s + 1]}
            new = dict(have)
            for at, group in enumerate(groups_of(GATHER, p, s)):
                needs = [t for o in group for t in have[slot_of("yxz", {**zero, **o})]]
                token = [("gather", p, s, at, k) for k in range(2)]
                add(("send", p, s, at), needs, 0.0, [(link, g * n * 512, token[0]) for link in links_of(d)], rank)
                found = {1: [token[0]]}
                if d != "z":
                    sends = [("+" + d, g * low * 512, token[1]), ("-" + d, g * (n - low) * 512, token[1])]
                    add(("pass", p, s, at), [token[0]], 0.0, sends, rank)
                    found = {3: [token[0]], 1: [token[0]], 2: [token[1]]}
                for k, tokens in found.items():
                    for o in group:
                        new[slot_of("yxz", {**zero, **o, d: k})] = tokens
            have = new
        for slot, tokens in have.items():
            arrivals[slot] += tokens
    for slot in range(32):
        add(("product", slot), arrivals[slot] + [("dot", k) for k in range(32)], PRODUCT, [], 90)

    add(("sum", 0), [], 0.0, [("core", SHARD * COLS * 2, ("sum", "in", 0))], 1)
    add(("sum", 1), [("sum", "in", 0)], 0.1, [("z", SHARD * COLS * 2, ("sum", "in", 1))], 11)
    add(("sum", 2), [("sum", "in", 1)], 0.1, [("core", SHARD * COLS * 2, ("sum", "in", 2))], 12)
    add(("update",), [("sum", "in", 2)] + [("final", p) for p in range(len(REDUCE))], 1.0, [], 80)
    return tasks


def in_order(tasks):
    now, done, free, order = 0.0, {}, {}, []
    left = sorted(tasks, key=lambda task: task[4])
    while left:
        ready, soonest = None, None
        for task in left:
            if task[4] == 30 and any(free.get(link, 0.0) > now + AHEAD for link, _, _ in task[3]):
                at = max(free.get(link, 0.0) - AHEAD for link, _, _ in task[3])
                soonest = at if soonest is None else min(soonest, at)
            elif all(token in done for token in task[1]):
                at = max([done[token] for token in task[1]], default=0.0)
                if at <= now:
                    ready = task
                    break
                soonest = at if soonest is None else min(soonest, at)
        if ready is None:
            now = soonest
            continue
        left.remove(ready)
        order.append(ready)
        now += ready[2]
        done[ready[0]] = now
        for link, size, token in ready[3]:
            rate = 12 * RATE if link == "core" else RATE
            free[link] = max(free.get(link, 0.0), now) + size / rate + MESSAGE
            done[token] = max(done.get(token, 0.0), free[link] + DELAY)
    return order


class Layout:
    def __init__(self):
        self.names, self.shapes = [], []

    def add(self, name, shape):
        self.names.append(name)
        self.shapes.append(shape)


def layout():
    own = Layout()
    own.add("grad", pltpu.VMEM((TOK, COLS), BF16))
    own.add("grad_t", pltpu.VMEM((COLS, TOK), BF16))
    own.add("mast", pltpu.VMEM((SHARD, COLS), F32))
    own.add("weight", pltpu.VMEM((4, 4, 2, COLS, SHARD), BF16))
    own.add("term", pltpu.VMEM((32, COLS, SHARD), F32))
    own.add("sum_send", pltpu.VMEM((SHARD // 2, COLS), F32))
    own.add("sum_recv", pltpu.VMEM((2, SHARD // 2, COLS), F32))
    own.add("sum", pltpu.VMEM((SHARD, COLS), F32))
    own.add("sum_ss", pltpu.SemaphoreType.DMA((3,)))
    own.add("sum_rs", pltpu.SemaphoreType.DMA((3,)))
    own.add("grad_sum", pltpu.VMEM((COLS, SHARD), F32))
    own.add("state", pltpu.VMEM((4, SHARD, COLS), F32))
    own.add("in_sem", pltpu.SemaphoreType.DMA((7,)))
    for p, (_, n, _, _, _) in enumerate(REDUCE):
        own.add(f"send{p}", pltpu.VMEM((31, n, SHARD), BF16))
        own.add(f"recv{p}", pltpu.VMEM((31, n, SHARD), BF16))
    for parts, one, two in ((REDUCE, "rs", "rr"), (GATHER, "gs", "gr")):
        for p in range(len(parts)):
            own.add(f"{one}{p}", pltpu.SemaphoreType.DMA)
            for s in range(3):
                own.add(f"{two}{p}{s}", pltpu.SemaphoreType.DMA((len(links_of(parts[p][3][s])), len(groups_of(parts, p, s)))))
    return own


def kernel(names, rows_hbm, grad_hbm, mast_hbm, first_hbm, second_hbm, anchor_hbm, outer_hbm, out_ref, *refs):
    new_master, new_first, new_second, new_anchor, new_outer = refs[:5]
    refs = refs[5:]
    ref = dict(zip(names, refs))
    rep, fsdp = lax.axis_index("rep"), lax.axis_index("fsdp")
    me = {"y": fsdp // 8, "x": fsdp // 2 % 4, "z": fsdp % 2}
    core = rep % 2
    place = {d: [(me[d] + k) % SIZE[d] for k in range(SIZE[d])] for d in "yxz"}

    def device(y, x, z):
        return (rep, (y * 4 + x) * 2 + z)

    to = {
        "+y": device(place["y"][1], me["x"], me["z"]),
        "-y": device(place["y"][3], me["x"], me["z"]),
        "+x": device(me["y"], place["x"][1], me["z"]),
        "-x": device(me["y"], place["x"][3], me["z"]),
        "z": device(me["y"], me["x"], place["z"][1]),
        "core": (rep + 1 - 2 * core, fsdp),
        "far": ((rep + 2) % 4, fsdp),
    }

    barrier = pltpu.get_barrier_semaphore()
    for target in to.values():
        pl.semaphore_signal(barrier, inc=1, device_id=target, device_id_type=MESH)

    mast_copy = pltpu.make_async_copy(mast_hbm, ref["mast"], ref["in_sem"].at[4])
    grad_copy = pltpu.make_async_copy(grad_hbm, ref["grad"], ref["in_sem"].at[5])
    row_copies = []
    for k in range(4):
        columns = pl.ds(pl.multiple_of(place["y"][(2, 1, 3, 0)[k]] * (8 * SHARD), 8 * SHARD), 8 * SHARD)
        row_copies.append(pltpu.make_async_copy(rows_hbm.at[:, columns], out_ref.at[:, columns], ref["in_sem"].at[k]))
    state_copies = []
    for k, hbm in enumerate((first_hbm, second_hbm, anchor_hbm, outer_hbm)):
        state_copies.append(pltpu.make_async_copy(hbm, ref["state"].at[k], ref["in_sem"].at[6]))
    mast_copy.start()
    grad_copy.start()

    def columns_of(o):
        y, x, z = [place[d][o[d]] for d in "yxz"]
        return pl.ds(pl.multiple_of(((y * 4 + x) * 2 + z) * SHARD, SHARD), SHARD)

    def remote(src, dst, send_sem, recv_sem, target):
        return pltpu.make_async_remote_copy(
            src_ref=src, dst_ref=dst, send_sem=send_sem, recv_sem=recv_sem, device_id=target, device_id_type=MESH
        )

    half = SHARD // 2
    mine = pl.ds(pl.multiple_of(core * half, half), half)
    other = pl.ds(pl.multiple_of((1 - core) * half, half), half)

    def sum_copy(k):
        src, dst, target = (
            (ref["mast"].at[other], ref["sum_recv"].at[0], to["core"]),
            (ref["sum_send"], ref["sum_recv"].at[1], to["far"]),
            (ref["sum"].at[mine], ref["sum"].at[mine], to["core"]),
        )[k]
        return remote(src, dst, ref["sum_ss"].at[k], ref["sum_rs"].at[k], target)

    def weight_at(d, at, group, first, count):
        index = []
        for e in "yxz":
            if e == d:
                index.append(at)
            elif e in group[0] and group[0][e] != group[-1][e]:
                index.append(pl.ds(group[0][e], len(group)))
            else:
                index.append(group[0].get(e, 0))
        return ref["weight"].at[(*index, pl.ds(first, count))]

    def gather_copy(p, s, at, kind):
        first, n, low, order, _ = GATHER[p]
        d = order[s]
        if d == "z":
            src, dst, a, c, link = 0, 1, first, n, "z"
        else:
            src, dst, a, c, link = (
                (0, 3, first, n, "+" + d),
                (0, 1, first, n, "-" + d),
                (3, 2, first, low, "+" + d),
                (1, 2, first + low, n - low, "-" + d),
            )[kind]
        group = groups_of(GATHER, p, s)[at]
        return remote(
            weight_at(d, src, group, a, c),
            weight_at(d, dst, group, a, c),
            ref[f"gs{p}"],
            ref[f"gr{p}{s}"].at[kind // 2, at],
            to[link],
        )

    def reduce_copy(p, s, at, kind):
        _, n, low, order, together = REDUCE[p]
        d = order[s]
        if d == "z":
            buf, a, c, link = 0, 0, n, "z"
        else:
            buf, a, c, link = (
                (0, 0, low, "+" + d),
                (0, low, n - low, "-" + d),
                (1, 0, n, "+" + d),
                (2, 0, n, "-" + d),
            )[kind]
        slots = pl.ds(block_of(p, s, buf, at * together[s]), together[s])
        return remote(
            ref[f"send{p}"].at[slots, pl.ds(a, c)],
            ref[f"recv{p}"].at[slots, pl.ds(a, c)],
            ref[f"rs{p}"],
            ref[f"rr{p}{s}"].at[kind // 2, at],
            to[link],
        )

    def gather_wait(p, s, at, phase):
        first, n, _, order, _ = GATHER[p]
        d, group = order[s], groups_of(GATHER, p, s)[at]
        where = 1 if d == "z" else 2 if phase else pl.ds(0, 2)
        block, sem = weight_at(d, where, group, first, n), ref[f"gr{p}{s}"].at[phase, at]
        remote(block, block, sem, sem, to["z"]).wait_recv()

    def reduce_wait(p, s, at, phase):
        _, n, _, order, together = REDUCE[p]
        g, sem = together[s], ref[f"rr{p}{s}"].at[phase, at]
        count = 2 * g if phase else g
        block = ref[f"recv{p}"].at[pl.ds(block_of(p, s, phase, at * g), count)]
        remote(block, block, sem, sem, to["z"]).wait_recv()

    waited = set()

    def wait_for(token):
        if token in waited or (token[0] not in ("reduce", "gather") and "in" not in token):
            return
        waited.add(token)
        if token[0] == "sum":
            sum_copy(token[2]).wait_recv()
        else:
            (reduce_wait if token[0] == "reduce" else gather_wait)(*token[1:])

    def term(p, s, o):
        first, n, _, order, _ = REDUCE[p]
        value = ref["term"][slot_of("yxz", o), first : first + n, :]
        for t in range(s):
            slot = slot_of(order[t + 1 :], o)
            for buf in (0,) if order[t] == "z" else (1, 2):
                value = value + ref[f"recv{p}"][block_of(p, t, buf, slot)].astype(F32)
        return value

    def do_dot(slot):
        o = SHARDS[slot]
        value = jnp.dot(ref["grad_t"][...], out_ref[:, columns_of(o)], preferred_element_type=F32)
        for p, (first, n, _, order, _) in enumerate(REDUCE):
            d = order[0]
            piece = value[first : first + n, :]
            if o[d] == (1 if d == "z" else 2):
                ref[f"send{p}"][slot_of(order[1:], o)] = piece.astype(BF16)
            else:
                ref["term"][slot, first : first + n, :] = piece

    def do_far(p, s, at):
        order = REDUCE[p][3]
        d = order[s]
        for inner in groups_of(REDUCE, p, s)[at] if s else ():
            o = {**{e: 0 for e in order[:s]}, **inner, d: 1 if d == "z" else 2}
            ref[f"send{p}"][block_of(p, s, 0, slot_of(order[s + 1 :], inner))] = term(p, s, o).astype(BF16)
        for kind in range(len(links_of(d))):
            reduce_copy(p, s, at, kind).start()

    def do_near(p, s, at):
        _, n, low, order, _ = REDUCE[p]
        send, recv = ref[f"send{p}"], ref[f"recv{p}"]
        for kind in (0, 1):
            for inner in groups_of(REDUCE, p, s)[at]:
                value = term(p, s, {**{e: 0 for e in order[:s]}, **inner, order[s]: 1 + 2 * kind})
                slot = slot_of(order[s + 1 :], inner)
                came, goes = block_of(p, s, 0, slot), block_of(p, s, kind + 1, slot)
                for which, (a, b) in enumerate(((0, low), (low, n))):
                    piece = value[a:b]
                    if which == kind:
                        piece = piece + recv[came, a:b].astype(F32)
                    send[goes, a:b] = piece.astype(BF16)
            reduce_copy(p, s, at, kind + 2).start()

    def do_final(p):
        first, n = REDUCE[p][:2]
        ref["grad_sum"][first : first + n, :] = term(p, 3, {"y": 0, "x": 0, "z": 0})

    def do_update():
        pltpu.make_async_copy(ref["state"], ref["state"], ref["in_sem"].at[6]).wait()

        gradient_t = ref["grad_sum"]
        for k in range(2):
            rows = slice(k * 128, k * 128 + 128)
            gradient = jnp.transpose(gradient_t[:, rows])
            master = ref["mast"][rows, :]
            first_new = beta_one * ref["state"][0, rows, :] + (1.0 - beta_one) * gradient
            second_new = beta_two * ref["state"][1, rows, :] + (1.0 - beta_two) * gradient * gradient
            update = first_new / bias_one / (jnp.sqrt(second_new / bias_two) + 1e-08)
            inner = master - 0.002 * (update + 0.1 * master)
            anchor = ref["state"][2, rows, :]
            delta = anchor - ref["sum"][rows, :] / 4.0
            outer_new = 0.9 * ref["state"][3, rows, :] + delta
            anchor_new = anchor - 0.7 * (0.9 * outer_new + delta)
            new_first[rows, :] = first_new
            new_second[rows, :] = second_new
            new_outer[rows, :] = outer_new
            new_anchor[rows, :] = anchor_new
            new_master[rows, :] = 0.5 * inner + 0.5 * anchor_new

    def do_send(p, s, at):
        for kind in range(len(links_of(GATHER[p][3][s]))):
            gather_copy(p, s, at, kind).start()

    def do_pass(p, s, at):
        gather_copy(p, s, at, 2).start()
        gather_copy(p, s, at, 3).start()

    def do_product(slot):
        value = jnp.dot(ref["grad"][...], ref["weight"][tuple(SHARDS[slot].values())], preferred_element_type=F32)
        out_ref[:, columns_of(SHARDS[slot])] = value.astype(BF16)

    def do_sum(k):
        if k == 1:
            ref["sum_send"][...] = ref["mast"][mine, :] + ref["sum_recv"][0]
        if k == 2:
            ref["sum"][mine, :] = ref["sum_send"][...] + ref["sum_recv"][1]
        if k < 3:
            sum_copy(k).start()

    steps = {
        "dot": do_dot,
        "far": do_far,
        "near": do_near,
        "final": do_final,
        "update": do_update,
        "send": do_send,
        "pass": do_pass,
        "product": do_product,
        "sum": do_sum,
    }

    mast_copy.wait()
    for copy in row_copies:
        copy.start()
    ref["weight"][0, 0, 0] = jnp.transpose(ref["mast"][...]).astype(BF16)
    pl.semaphore_wait(barrier, len(to))

    row_order = (2, 1, 3, 0)
    loaded = set()
    for name, needs, _, _, _ in in_order(make_tasks()):
        if name[0] == "dot":
            if not loaded:
                grad_copy.wait()
                ref["grad_t"][...] = jnp.transpose(ref["grad"][...].astype(F32)).astype(BF16)
            y = SHARDS[name[1]]["y"]
            if y not in loaded:
                loaded.add(y)
                row_copies[row_order.index(y)].wait()
                if len(loaded) == 4:
                    for copy in state_copies:
                        copy.start()
        for token in needs:
            wait_for(token)
        with jax.named_scope(name[0]):
            steps[name[0]](*name[1:])

    end = jax.named_scope("left")
    end.__enter__()
    for p in range(len(REDUCE)):
        for sem in (ref[f"rs{p}"], ref[f"gs{p}"]):
            remote(ref[f"send{p}"], ref[f"recv{p}"], sem, sem, to["z"]).wait_send()
    for k in range(3):
        sum_copy(k).wait_send()
    end.__exit__(None, None, None)


def write_out(*refs):
    count = len(refs) // 2
    sem = refs[-1]
    copies = []
    for k in range(count):
        src, dst = refs[k], refs[count + k]
        cuts = 8 if k == 0 else 1
        rows = src.shape[0] // cuts
        for c in range(cuts):
            part = pl.ds(c * rows, rows)
            copies.append(pltpu.make_async_copy(src.at[part], dst.at[part], sem.at[len(copies)]))
    for copy in copies:
        copy.start()
    for copy in copies:
        copy.wait()


def exchange(*args):
    own = layout()
    shapes = [((TOK, 32 * SHARD), BF16)] + [((SHARD, COLS), F32)] * 5
    results = pl.pallas_call(
        functools.partial(kernel, tuple(own.names)),
        out_shape=[pltpu.VMEM(*shape) for shape in shapes],
        in_specs=[pl.BlockSpec(memory_space=pltpu.HBM)] * 7,
        out_specs=[pl.BlockSpec(memory_space=pltpu.VMEM)] * 6,
        scratch_shapes=own.shapes,
        compiler_params=pltpu.CompilerParams(collective_id=0, has_side_effects=True, vmem_limit_bytes=53 << 20),
        cost_estimate=pl.CostEstimate(flops=2 * 2 * TOK * COLS * 32 * SHARD, bytes_accessed=20 << 20, transcendentals=0),
    )(*args)
    return pl.pallas_call(
        write_out,
        out_shape=[jax.ShapeDtypeStruct(*shape) for shape in shapes],
        in_specs=[pl.BlockSpec(memory_space=pltpu.VMEM)] * 6,
        out_specs=[pl.BlockSpec(memory_space=pltpu.HBM)] * 6,
        scratch_shapes=[pltpu.SemaphoreType.DMA((13,))],
        compiler_params=pltpu.CompilerParams(vmem_limit_bytes=4 << 20),
    )(*[pltpu.with_memory_space_constraint(r, pltpu.VMEM) for r in results])


def on_device(layer_input, out_grad, master, first_moment, second_moment, anchor, outer_moment):
    input_grad, master_new, first_new, second_new, anchor_new, outer_new = exchange(
        layer_input, out_grad, master[0], first_moment[0], second_moment[0], anchor, outer_moment
    )
    return (input_grad, master_new[None], first_new[None], second_new[None], anchor_new, outer_new)


def solution(mesh):
    return jax.shard_map(
        on_device,
        mesh=mesh,
        in_specs=(
            P(("rep", "fsdp"), None),
            P(("rep", "fsdp"), None),
            P("rep", "fsdp", None),
            P("rep", "fsdp", None),
            P("rep", "fsdp", None),
            P("fsdp", None),
            P("fsdp", None),
        ),
        out_specs=(
            P(("rep", "fsdp"), None),
            P("rep", "fsdp", None),
            P("rep", "fsdp", None),
            P("rep", "fsdp", None),
            P("fsdp", None),
            P("fsdp", None),
        ),
        check_vma=False,
    )
```

time: 90.4 us -> 88.3 us (0.977)
  local copies, waits for them, and re-layouts: 3.68 us -> 0 us
  Pallas kernels: 84.2 us -> 87.4 us
  other arithmetic: 1.71 us -> 0 us
    unnamed x11 -> x0, local copies, waits for them, and re-layouts: 3.68 us -> none
    pallas_call x1 -> x2, Pallas kernels: 84.2 us -> 87.4 us  [the longest x1 83.2 us: exchange(): pl.pallas_call(functools.partial(kernel, tuple(own.names)), out_shape=[pl...]
    broadcast_in_dim x1 -> x0, other arithmetic: 1.71 us -> none  [on_device(): master_new[None]]
where the time goes in v3:
time: 88.3 us; the launch traced here: 88.2 us
  Pallas kernels  87.4 us (99%)
    pallas_call x1, Pallas kernels, exchange(): pl.pallas_call(functools.partial(kernel, tuple(own.names)), out_shape=[pl...  83.2 us
    pallas_call x1, Pallas kernels, exchange(): pl.pallas_call(write_out, out_shape=[jax.ShapeDtypeStruct(*shape) for sha...  4.18 us

profile of v3, /device:TPU:0, one launch (start us, length us, event | category | flops | bytes accessed | tf_op | source)
XLA Modules:
  0.0 88.2 jit_solution(1865885517894151533)
XLA Ops:
  0.6 83.2 %shard_map.118 = (bf16[512,8192]{1,0:T(8,128)(2,1)S(1)}, f32[256,512]{1,0:T(8,128)S(1)}, f32[256,512]{1,0:T(8,128)S(1)}, f32[256,512]{1,0:T(8,128)S(1)}, f32[256,512]{1,0:T(8,128)S(1)}, /*index=5*/f32[256,512]{1,0:T(8,128)S(1)}) custom-call(bf16[512,8192]{1,0:T(8,128)(2,1)} %rows_hbm.1, bf16[512,512]{1,0:T(8,128)(2,1)} %grad_hbm.1, f32[256,512]{1,0:T(8,128)} %bitcast.6, ...), custom_call_target="tpu_custom_call" | custom-call | flops 8589934592 | bytes 20971520 | tf_op jit(solution)/shard_map/pallas_call | solution.py:507
  83.8 4.2 %shard_map.119 = (bf16[512,8192]{1,0:T(8,128)(2,1)}, f32[256,512]{1,0:T(8,128)}, f32[256,512]{1,0:T(8,128)}, f32[256,512]{1,0:T(8,128)}, f32[256,512]{1,0:T(8,128)}, /*index=5*/f32[256,512]{1,0:T(8,128)}) custom-call(bf16[512,8192]{1,0:T(8,128)(2,1)S(1)} %get-tuple-element.18.refs_0_, f32[256,512]{1,0:T(8,128)S(1)} %get-tuple-element.19.refs_1_, ...), custom_call_target="tpu_custom_call" | custom-call | tf_op jit(solution)/shard_map/pallas_call | solution.py:516

commit v4 on v3

--- a/solution.py
+++ b/solution.py
@@ -31,13 +31,19 @@
 GATHER = (
     (0, 176, 80, "yxz", (2, 1, 1)),
     (176, 176, 96, "xyz", (2, 1, 1)),
-    (352, 80, 48, "zyx", (4, 1, 1)),
-    (432, 80, 32, "zxy", (4, 1, 1)),
+    (352, 80, 48, "zyx", (4, 2, 1)),
+    (432, 80, 32, "zxy", (4, 2, 1)),
 )
 
-RATE, MESSAGE, DELAY = 48500.0, 0.08, 1.5
+RATE, MESSAGE, DELAY = 48448.7, 0.05, 2.271
 DOT, PRODUCT, ADD, SEND = 0.40, 0.38, 0.0005, 0.02
-AHEAD = 6.0
+AHEAD = 3.042
+RANK = {
+    "far": ((3.47, 14.97, 17.22), (-2.73, 34.93, 2.84)),
+    "near": ((6.27, 21.7, 10.27), (31.86, 16.78, 25.62)),
+    "send": ((12.08, 3.9, 9.83), (32.06, 7.23, 0.08)),
+    "pass": ((25.72, 22.74, 16.64), (20.22, 7.85, 10.75)),
+}
 
 
 def count_of(dims):
@@ -86,6 +92,8 @@
     tasks = []
 
     def add(name, needs, time, sends, rank):
+        if name[0] in RANK:
+            rank = RANK[name[0]][name[1] // 2][name[2]]
         tasks.append((name, tuple(dict.fromkeys(needs)), time + SEND * len(sends), tuple(sends), rank))
 
     def term_needs(p, s, o):
@@ -152,7 +160,7 @@
     while left:
         ready, soonest = None, None
         for task in left:
-            if task[4] == 30 and any(free.get(link, 0.0) > now + AHEAD for link, _, _ in task[3]):
+            if task[0][0] in ("send", "pass") and task[0][2] == 0 and any(free.get(link, 0.0) > now + AHEAD for link, _, _ in task[3]):
                 at = max(free.get(link, 0.0) - AHEAD for link, _, _ in task[3])
                 soonest = at if soonest is None else min(soonest, at)
             elif all(token in done for token in task[1]):
@@ -162,7 +170,7 @@
                     break
                 soonest = at if soonest is None else min(soonest, at)
         if ready is None:
-            now = soonest
+            now = max(soonest, now + 0.001)
             continue
         left.remove(ready)
         order.append(ready)
@@ -275,7 +283,7 @@
             if e == d:
                 index.append(at)
             elif e in group[0] and group[0][e] != group[-1][e]:
-                index.append(pl.ds(group[0][e], len(group)))
+                index.append(pl.ds(group[0][e], group[-1][e] - group[0][e] + 1))
             else:
                 index.append(group[0].get(e, 0))
         return ref["weight"].at[(*index, pl.ds(first, count))]
@@ -474,14 +482,11 @@
         with jax.named_scope(name[0]):
             steps[name[0]](*name[1:])
 
-    end = jax.named_scope("left")
-    end.__enter__()
     for p in range(len(REDUCE)):
         for sem in (ref[f"rs{p}"], ref[f"gs{p}"]):
             remote(ref[f"send{p}"], ref[f"recv{p}"], sem, sem, to["z"]).wait_send()
     for k in range(3):
         sum_copy(k).wait_send()
-    end.__exit__(None, None, None)
 
 
 def write_out(*refs):

time: 88.3 us -> 85.7 us (0.971)
  Pallas kernels: 87.4 us -> 84.8 us
    pallas_call x1, Pallas kernels: 83.2 us -> 80.6 us  [exchange(): pl.pallas_call(functools.partial(kernel, tuple(own.names)), out_shape=[pl...]
where the time goes in v4:
time: 85.7 us; the launch traced here: 85.6 us
  Pallas kernels  84.8 us (99%)
    pallas_call x1, Pallas kernels, exchange(): pl.pallas_call(functools.partial(kernel, tuple(own.names)), out_shape=[pl...  80.6 us
    pallas_call x1, Pallas kernels, exchange(): pl.pallas_call(write_out, out_shape=[jax.ShapeDtypeStruct(*shape) for sha...  4.18 us

profile of v4, /device:TPU:0, one launch (start us, length us, event | category | flops | bytes accessed | tf_op | source)
XLA Modules:
  0.0 85.6 jit_solution(2396408093111079110)
XLA Ops:
  0.6 80.6 %shard_map.118 = (bf16[512,8192]{1,0:T(8,128)(2,1)S(1)}, f32[256,512]{1,0:T(8,128)S(1)}, f32[256,512]{1,0:T(8,128)S(1)}, f32[256,512]{1,0:T(8,128)S(1)}, f32[256,512]{1,0:T(8,128)S(1)}, /*index=5*/f32[256,512]{1,0:T(8,128)S(1)}) custom-call(bf16[512,8192]{1,0:T(8,128)(2,1)} %rows_hbm.1, bf16[512,512]{1,0:T(8,128)(2,1)} %grad_hbm.1, f32[256,512]{1,0:T(8,128)} %bitcast.6, ...), custom_call_target="tpu_custom_call" | custom-call | flops 8589934592 | bytes 20971520 | tf_op jit(solution)/shard_map/pallas_call | solution.py:512
  81.2 4.2 %shard_map.119 = (bf16[512,8192]{1,0:T(8,128)(2,1)}, f32[256,512]{1,0:T(8,128)}, f32[256,512]{1,0:T(8,128)}, f32[256,512]{1,0:T(8,128)}, f32[256,512]{1,0:T(8,128)}, /*index=5*/f32[256,512]{1,0:T(8,128)}) custom-call(bf16[512,8192]{1,0:T(8,128)(2,1)S(1)} %get-tuple-element.18.refs_0_, f32[256,512]{1,0:T(8,128)S(1)} %get-tuple-element.19.refs_1_, ...), custom_call_target="tpu_custom_call" | custom-call | tf_op jit(solution)/shard_map/pallas_call | solution.py:521

commit v5 on v4

--- a/solution.py
+++ b/solution.py
@@ -434,8 +434,9 @@
         gather_copy(p, s, at, 3).start()
 
     def do_product(slot):
-        value = jnp.dot(ref["grad"][...], ref["weight"][tuple(SHARDS[slot].values())], preferred_element_type=F32)
-        out_ref[:, columns_of(SHARDS[slot])] = value.astype(BF16)
+        for rows in (slice(0, 256), slice(256, 512)):
+            value = jnp.dot(ref["grad"][rows, :], ref["weight"][tuple(SHARDS[slot].values())], preferred_element_type=F32)
+            out_ref[rows, columns_of(SHARDS[slot])] = value.astype(BF16)
 
     def do_sum(k):
         if k == 1:

time: 85.7 us -> 85.2 us (level)
  no operation moved by 1% of the time
where the time goes in v5:
time: 85.2 us; the launch traced here: 85.1 us
  Pallas kernels  84.5 us (99%)
    pallas_call x1, Pallas kernels, exchange(): pl.pallas_call(functools.partial(kernel, tuple(own.names)), out_shape=[pl...  80.3 us
    pallas_call x1, Pallas kernels, exchange(): pl.pallas_call(write_out, out_shape=[jax.ShapeDtypeStruct(*shape) for sha...  4.18 us

profile of v5, /device:TPU:0, one launch (start us, length us, event | category | flops | bytes accessed | tf_op | source)
XLA Modules:
  0.0 85.1 jit_solution(5838516109356057547)
XLA Ops:
  0.6 80.3 %shard_map.118 = (bf16[512,8192]{1,0:T(8,128)(2,1)S(1)}, f32[256,512]{1,0:T(8,128)S(1)}, f32[256,512]{1,0:T(8,128)S(1)}, f32[256,512]{1,0:T(8,128)S(1)}, f32[256,512]{1,0:T(8,128)S(1)}, /*index=5*/f32[256,512]{1,0:T(8,128)S(1)}) custom-call(bf16[512,8192]{1,0:T(8,128)(2,1)} %rows_hbm.1, bf16[512,512]{1,0:T(8,128)(2,1)} %grad_hbm.1, f32[256,512]{1,0:T(8,128)} %bitcast.6, ...), custom_call_target="tpu_custom_call" | custom-call | flops 8589934592 | bytes 20971520 | tf_op jit(solution)/shard_map/pallas_call | solution.py:513
  80.9 4.2 %shard_map.119 = (bf16[512,8192]{1,0:T(8,128)(2,1)}, f32[256,512]{1,0:T(8,128)}, f32[256,512]{1,0:T(8,128)}, f32[256,512]{1,0:T(8,128)}, f32[256,512]{1,0:T(8,128)}, /*index=5*/f32[256,512]{1,0:T(8,128)}) custom-call(bf16[512,8192]{1,0:T(8,128)(2,1)S(1)} %get-tuple-element.18.refs_0_, f32[256,512]{1,0:T(8,128)S(1)} %get-tuple-element.19.refs_1_, ...), custom_call_target="tpu_custom_call" | custom-call | tf_op jit(solution)/shard_map/pallas_call | solution.py:522
